TPU v7x, 32 devices: a whole 2x2x4 slice. The times are simulated.
32 devices in a mesh: ctx: 8 (over z, x), tp: 4 (over y, core).
Axes of the slice: x: 2, y: 2, z: 4, core: 2. Of those that a mesh axis runs over, the one named last changes fastest.
Arguments:
- hidden_in: bfloat16 [4096, 4096], P('ctx', 'tp'), may hold values from -6 to 6
- norm_gain: bfloat16 [1, 4096], P(None, 'ctx'), may hold values from 0.25 to 1.75
- w_qkv: bfloat16 [1, 3, 4096, 512], P(None, None, 'ctx', 'tp'), may hold values from -0.09375 to 0.09375
- w_out: bfloat16 [1, 512, 4096], P(None, 'tp', 'ctx'), may hold values from -1 to 1
Outputs:
- hidden_out: bfloat16 [4096, 4096], P('ctx', 'tp')
All inputs are finite; a program needn't handle non-finite values.
Results may differ from a plain program's by a relative error of at most 0.015.
Values may be sent and summed in bfloat16 or wider, within the bound.
A program may use at most 64 MiB of HBM per device.

v0:
```python
import math

import jax
import jax.numpy as jnp
from jax import lax
from jax.sharding import PartitionSpec as P

HD = 128


def shifted(value, axis, by):
    devices = lax.axis_size(axis)
    pairs = [(i, i + by) for i in range(devices) if 0 <= i + by < devices]
    return lax.ppermute(value, axis, pairs)


def normalize(hidden):
    values = hidden.astype(jnp.float32)
    return values * lax.rsqrt(jnp.mean(values * values, axis=-1, keepdims=True) + 1e-06)


def scaled(source, piece_g):
    return (source * piece_g.astype(jnp.float32)).astype(jnp.bfloat16)


def project_rows(normed_own, weights, row_gain):
    piece_w = lax.all_gather(weights, "ctx", axis=1, tiled=True)
    piece_g = lax.all_gather(row_gain, "ctx", axis=1, tiled=True)
    inputs = scaled(normed_own, piece_g)
    return (jnp.einsum("rd,cdh->crh", inputs, piece_w, preferred_element_type=jnp.float32),)


def attend(queries, key_rows, value_rows, mem_keys, mem_values, owner_index, score_scale):
    seg_rows = queries.shape[0]
    all_keys = jnp.concatenate([mem_keys, key_rows], axis=0)
    all_values = jnp.concatenate([mem_values, value_rows], axis=0)
    scores = (
        jnp.einsum("qd,kd->qk", queries, all_keys, preferred_element_type=jnp.float32) * score_scale
    )
    row_ids = lax.broadcasted_iota(jnp.int32, scores.shape, 0)
    col_ids = lax.broadcasted_iota(jnp.int32, scores.shape, 1)
    allowed = jnp.where(col_ids < seg_rows, owner_index > 0, col_ids - seg_rows <= row_ids)
    exp_scores = jnp.where(allowed, jnp.exp(scores), 0.0)
    probs = (exp_scores / jnp.sum(exp_scores, axis=1, keepdims=True)).astype(jnp.bfloat16)
    return jnp.dot(probs, all_values, preferred_element_type=jnp.float32).astype(jnp.bfloat16)


def per_device(hidden_in, norm_gain, w_qkv, w_out):
    owner_index = lax.axis_index("ctx")
    score_scale = 1.0 / math.sqrt(HD)
    hidden = hidden_in
    weights = w_qkv[0]
    row_gain = norm_gain[0][None, :]
    whole_own = lax.all_gather(hidden, "tp", axis=1, tiled=True)
    own_proj = project_rows(normalize(whole_own), weights, row_gain)[0].astype(jnp.bfloat16)
    mem_pair = shifted(own_proj[1:], "ctx", 1)
    attended = attend(
        own_proj[0], own_proj[1], own_proj[2], mem_pair[0], mem_pair[1], owner_index, score_scale
    )
    partials = jnp.dot(
        attended,
        lax.all_gather(w_out[0], "ctx", axis=1, tiled=True),
        preferred_element_type=jnp.float32,
    )
    summed = lax.psum_scatter(
        partials.astype(jnp.bfloat16), "tp", scatter_dimension=1, tiled=True
    ).astype(jnp.float32)
    hidden = (hidden.astype(jnp.float32) + summed).astype(jnp.bfloat16)
    return hidden


def solution(mesh):
    placed = (P("ctx", "tp"), P(None, "ctx"), P(None, None, "ctx", "tp"), P(None, "tp", "ctx"))
    return jax.shard_map(
        per_device, mesh=mesh, in_specs=placed, out_specs=P("ctx", "tp"), check_vma=False
    )
```

profile of v0, /device:TPU:31, one launch (start us, length us, event | category | flops | bytes accessed | tf_op | source)
XLA Modules:
  0.0 206.0 jit_solution(14216144961048485968)
XLA Ops:
  6.5 0.0 all-gather.6.cloned.1.call-start
  6.5 0.7 all-gather.6.cloned.1.call-update
  7.3 0.0 all-gather.8.cloned.1.call-start
  7.3 0.7 all-gather.8.cloned.1.call-update
  8.0 0.0 all-gather.10.cloned.1.call-start
  8.1 0.7 all-gather.10.cloned.1.call-update
  8.7 0.0 reduce-scatter.2.cloned.1.call-start
  8.8 20.5 %all_gather.13 = bf16[1,4096]{1,0:T(2,128)(2,1)S(1)} all-gather(bf16[1,512]{1,0:T(2,128)(2,1)} %param.5), channel_id=1, replica_groups=mesh['ctx'=8,'tp'=4] {'ctx'}, dimensions={1}, use_global_device_ids=true | all-gather | bytes 9216 | tf_op jit(solution)/shard_map/all_gather | solution.py:28
  29.4 14.5 %all-gather.6.cloned.1.call-done = bf16[512,4096]{1,0:T(8,128)(2,1)} async-done(((bf16[512,1024]{1,0:T(8,128)(2,1)}), bf16[512,4096]{1,0:T(8,128)(2,1)}) %all-gather.6.cloned.1.call-update) | async-done | bytes 4194320 | tf_op jit(solution)/shard_map/all_gather | solution.py:54
  43.8 3.1 %fusion = f32[512]{0:T(512)S(1)} fusion(bf16[512,4096]{1,0:T(8,128)(2,1)} %all-gather.6.cloned.1.call-done), kind=kLoop, calls=%fused_computation.2 | loop fusion | flops 6290944 | bytes 4196352 | tf_op jit(solution)/shard_map/reduce_sum | solution.py:19
  46.9 57.9 %all-gather.8.cloned.1.call-done = bf16[1,3,4096,128]{3,2,1,0:T(8,128)(2,1)} async-done(((bf16[1,3,512,128]{3,2,1,0:T(8,128)(2,1)}), bf16[1,3,4096,128]{3,2,1,0:T(8,128)(2,1)}) %all-gather.8.cloned.1.call-update) | async-done | bytes 3145744 | tf_op jit(solution)/shard_map/all_gather | solution.py:27
  104.8 5.5 %fusion.15 = bf16[3,512,128]{2,1,0:T(8,128)(2,1)S(1)} fusion(bf16[1,3,4096,128]{3,2,1,0:T(8,128)(2,1)} %all-gather.8.cloned.1.call-done, bf16[512,4096]{1,0:T(8,128)(2,1)} %all-gather.6.cloned.1.call-done, f32[4096]{0:T(1024)S(1)} %bitcast.33, f32[512]{0:T(512)S(1)} %add_rsqrt_fusion), kind=kOutput, calls=%fused_computation.17 | convolution fusion | flops 1619197952 | bytes 7751680 | tf_op jit(solution)/shard_map/rd,cdh->crh/dot_general | solution.py:30
  110.4 1.3 collective-permute-start
  111.8 9.2 %collective-permute-done = bf16[2,512,128]{2,1,0:T(8,128)(2,1)S(1)} collective-permute-done((bf16[2,512,128]{2,1,0:T(8,128)(2,1)S(1)}, bf16[2,512,128]{2,1,0:T(8,128)(2,1)S(1)}, u32[]{:S(2)}, u32[]{:S(2)}) %collective-permute-start) | collective-permute-done | bytes 262176 | tf_op jit(solution)/shard_map/ppermute | solution.py:14
  121.0 0.9 fusion.33
  121.9 23.7 %all-gather.10.cloned.1.call-done = bf16[1,128,4096]{2,1,0:T(8,128)(2,1)} async-done(((bf16[1,128,512]{2,1,0:T(8,128)(2,1)}), bf16[1,128,4096]{2,1,0:T(8,128)(2,1)}) %all-gather.10.cloned.1.call-update) | async-done | bytes 1048592 | tf_op jit(solution)/shard_map/all_gather | solution.py:62
  145.6 5.3 %convolution_convert_fusion = bf16[512,4096]{1,0:T(8,128)(2,1)} fusion(bf16[1,128,4096]{2,1,0:T(8,128)(2,1)} %all-gather.10.cloned.1.call-done, f32[512,1024]{1,0:T(8,128)S(1)} %get-tuple-element.10, f32[512]{0:T(512)S(1)} %get-tuple-element.9, bf16[512,128]{1,0:T(8,128)(2,1)S(1)} %get-tuple-element.5, bf16[512,128]{1,0:T(8,128)(2,1)S(1)} %get-tuple-element.7), kind=kOutput, calls=%fused_computation.5 | convolution fusion | flops 674824192 | bytes 7604224 | tf_op jit(solution)/shard_map/dot_general | solution.py:60
  150.9 0.0 copy-start
  150.9 0.0 reduce-scatter.2.cloned.1.call-update
  150.9 46.0 %reduce-scatter.2.cloned.1.call-done = bf16[512,1024]{1,0:T(8,128)(2,1)} async-done(((bf16[512,4096]{1,0:T(8,128)(2,1)}), bf16[512,1024]{1,0:T(8,128)(2,1)}) %reduce-scatter.2.cloned.1.call-update) | async-done | bytes 1048592 | tf_op jit(solution)/shard_map/reduce_scatter | solution.py:65
  196.9 0.0 copy-done
  196.9 2.6 %add_convert_fusion = bf16[512,1024]{1,0:T(8,128)(2,1)} fusion(bf16[512,1024]{1,0:T(8,128)(2,1)} %reduce-scatter.2.cloned.1.call-done, bf16[512,1024]{1,0:T(8,128)(2,1)S(1)} %copy-done), kind=kLoop, calls=%fused_computation.11 | loop fusion | flops 2097152 | bytes 3145728 | tf_op jit(solution)/shard_map/convert_element_type | solution.py:68
  (7 shorter events, 0.1 us)
Async XLA Ops:
  6.5 37.3 %all-gather.6.cloned.1.call-start = ((), (), s32[]{:S(2)}) async-start(), calls=%async_computation.1 | async-start | bytes 5242880 | tf_op jit(solution)/shard_map/all_gather | solution.py:54
  7.3 97.6 %all-gather.8.cloned.1.call-start = ((), (), s32[]{:S(2)}) async-start(), calls=%async_computation.3 | async-start | bytes 3538944 | tf_op jit(solution)/shard_map/all_gather | solution.py:27
  8.0 137.6 %all-gather.10.cloned.1.call-start = ((), (), s32[]{:S(2)}) async-start(), calls=%async_computation.4 | async-start | bytes 1179648 | tf_op jit(solution)/shard_map/all_gather | solution.py:62
  8.7 188.2 %reduce-scatter.2.cloned.1.call-start = ((), (), s32[]{:S(2)}) async-start(), calls=%async_computation.2 | async-start | bytes 5242880 | tf_op jit(solution)/shard_map/reduce_scatter | solution.py:65
  110.4 10.6 %collective-permute-start = (bf16[2,512,128]{2,1,0:T(8,128)(2,1)S(1)}, bf16[2,512,128]{2,1,0:T(8,128)(2,1)S(1)}, u32[]{:S(2)}, u32[]{:S(2)}) collective-permute-start(bf16[2,512,128]{2,1,0:T(8,128)(2,1)S(1)} %slice.25), channel_id=1, source_target_pairs={{0,4},{4,8},{8,12},{12,16},{16,20},{20,24},{24,28},{1,5},{5,9},{9,... | collective-permute-start | bytes 786440 | tf_op jit(solution)/shard_map/ppermute | solution.py:14
  150.9 46.0 %copy-start = (bf16[512,1024]{1,0:T(8,128)(2,1)S(1)}, bf16[512,1024]{1,0:T(8,128)(2,1)}, u32[]{:S(2)}) copy-start(bf16[512,1024]{1,0:T(8,128)(2,1)} %param.4) | copy-start | bytes 3145732
Sparse Core Ops, SparseCore 0:
  8.9 34.8 all-gather.5
  46.0 58.7 all-gather.7
  106.9 38.7 all-gather.9
  151.1 45.8 reduce-scatter.1
where the time goes:
time: 209 us; the launch traced here: 206 us
  waiting for transfers between devices  153 us (73%)
  blocking collectives  20.5 us (10%)
  between operations  13.2 us (6%)
  matrix products  11.7 us (6%)
  other arithmetic  5.71 us (3%)
    all_gather x1, waiting for transfers between devices, project_rows(): piece_w = lax.all_gather(weights, 'ctx', axis=1, tiled=True)  57.9 us
    reduce_scatter x1, waiting for transfers between devices, per_device(): lax.psum_scatter(partials.astype(jnp.bfloat16), 'tp', scatter_dimension=1...  46 us
    all_gather x1, waiting for transfers between devices, per_device(): lax.all_gather(w_out[0], 'ctx', axis=1, tiled=True)  23.7 us
    all_gather x1, blocking collectives, project_rows(): piece_g = lax.all_gather(row_gain, 'ctx', axis=1, tiled=True)  20.5 us
    all_gather x1, waiting for transfers between devices, per_device(): whole_own = lax.all_gather(hidden, 'tp', axis=1, tiled=True)  14.5 us
    ppermute x1, waiting for transfers between devices, shifted(): return lax.ppermute(value, axis, pairs)  9.21 us
    dot_general x1, matrix products, project_rows(): jnp.einsum('rd,cdh->crh', inputs, piece_w, preferred_element_type=jnp.flo...  5.54 us
    dot_general x1, matrix products, per_device(): jnp.dot(attended, lax.all_gather(w_out[0], 'ctx', axis=1, tiled=True), pr...  5.26 us
  transfers between devices with their start and end apart: 5, of which 5 were waited for; matrix products, arithmetic and copies ran while one was open for 5% of the time, Pallas kernels for 0%

commit v1 on v0

v1 whole, which is shorter than its diff:
```python
import functools
import math

import jax
import jax.numpy as jnp
from jax import lax
from jax.experimental import pallas as pl
from jax.experimental.pallas import tpu as pltpu
from jax.sharding import PartitionSpec as P

HD = 128
PAIR = 2
HIDDEN_CHUNKS = 2
KINDS = (1, 2, 0)


def kernel(
    n_ctx, n_tp,
    hid_ref, gain_ref, w_ref, o_ref, out_ref,
    hbuf, wbuf, obuf, wouse, kv, mem, qbuf, att, scale,
    w_recv, w_send, ol_recv, ol_send, ot_recv, ot_send, ox_recv, ox_send,
    h_recv, hs_send, hy_send, hf_send, kv_recv, kv_send, a_recv, a_send,
):
    line = n_ctx // PAIR
    n_y = n_tp // 2
    c = lax.axis_index("ctx")
    t = lax.axis_index("tp")
    a = lax.div(c, PAIR)
    b = lax.rem(c, PAIR)
    y = lax.div(t, 2)
    core = lax.rem(t, 2)
    seg, own_d = hid_ref.shape
    depth = w_ref.shape[1]
    rows_c = seg // HIDDEN_CHUNKS
    pair_c = PAIR * a + (1 - b)
    sib = 2 * y + (1 - core)
    has_right = a + 1 < line
    has_left = a >= 1

    def remote(src, dst, send, recv, ctx=None, tp=None):
        where = {}
        if ctx is not None:
            where["ctx"] = ctx
        if tp is not None:
            where["tp"] = tp
        return pltpu.make_async_remote_copy(
            src_ref=src, dst_ref=dst, send_sem=send, recv_sem=recv,
            device_id=where, device_id_type=pl.DeviceIdType.MESH,
        )

    barrier = pltpu.get_barrier_semaphore()

    def greet(**where):
        pl.semaphore_signal(barrier, inc=1, device_id=where, device_id_type=pl.DeviceIdType.MESH)

    greet(ctx=pair_c)
    for p in range(n_tp):
        @pl.when(p != t)
        def _():
            greet(tp=p)

    @pl.when(has_right)
    def _():
        greet(ctx=c + PAIR)

    @pl.when(has_left)
    def _():
        greet(ctx=c - PAIR)

    @pl.when((b == 1) & (c + 1 < n_ctx))
    def _():
        greet(ctx=c + 1)

    @pl.when((b == 0) & (c > 0))
    def _():
        greet(ctx=c - 1)

    gain = jnp.transpose(jnp.broadcast_to(gain_ref[...].astype(jnp.float32), (HD, depth)))
    for kind in KINDS:
        wbuf[kind, c] = (w_ref[kind].astype(jnp.float32) * gain).astype(jnp.bfloat16)
    obuf[a] = o_ref[...]
    hbuf[t] = hid_ref[...]

    @pl.when(c == 0)
    def _():
        mem[...] = jnp.zeros_like(mem)

    total = n_tp + has_right.astype(jnp.int32) + has_left.astype(jnp.int32)
    total += ((b == 1) & (c + 1 < n_ctx)).astype(jnp.int32)
    total += ((b == 0) & (c > 0)).astype(jnp.int32)
    pl.semaphore_wait(barrier, total)

    def h_part(slot, i):
        return hbuf.at[slot, pl.ds(i * rows_c, rows_c), :]

    def h_copy(slot, i, send, dest):
        part = h_part(slot, i)
        return remote(part, part, send, h_recv.at[slot, i], tp=dest)

    for i in range(HIDDEN_CHUNKS):
        for q in range(n_y):
            @pl.when(q != y)
            def _():
                h_copy(t, i, hy_send.at[q, i], 2 * q + core).start()

    def w_copy(kind, pa, way):
        pc = PAIR * pa + b
        slot = wbuf.at[kind, pc]
        dest = (c + PAIR, c - PAIR, pair_c)[way]
        return remote(slot, slot, w_send.at[kind, pa, way], w_recv.at[kind, pc], ctx=dest)

    def o_line(pa, way):
        slot = obuf.at[pa]
        dest = (c + PAIR, c - PAIR)[way]
        return remote(slot, slot, ol_send.at[pa, way], ol_recv.at[pa], ctx=dest)

    def o_tp(pa):
        dst = wouse.at[b, pl.ds(pl.multiple_of(t * HD, HD), HD), :]
        return remote(obuf.at[pa], dst, ot_send.at[pa], ot_recv.at[t], tp=pa)

    def o_pair(head):
        part = wouse.at[b, pl.ds(pl.multiple_of(head * HD, HD), HD), :]
        return remote(part, part, ox_send.at[head], ox_recv.at[head], ctx=pair_c)

    def own_sends(kind):
        @pl.when(has_right)
        def _():
            w_copy(kind, a, 0).start()

        @pl.when(has_left)
        def _():
            w_copy(kind, a, 1).start()

        w_copy(kind, a, 2).start()

    def own_o():
        @pl.when(has_right)
        def _():
            o_line(a, 0).start()

        @pl.when(has_left)
        def _():
            o_line(a, 1).start()

        o_route(a)

    def o_route(pa):
        @pl.when(pa == t)
        def _():
            wouse[b, pl.ds(pl.multiple_of(t * HD, HD), HD), :] = obuf[pa]
            o_pair(t).start()

        @pl.when(pa != t)
        def _():
            o_tp(pa).start()

    def w_wait(kind, pc):
        slot = wbuf.at[kind, pc]
        remote(slot, slot, w_send.at[kind, 0, 0], w_recv.at[kind, pc], ctx=pair_c).wait_recv()

    def pass_on(kind):
        def body(d, carry):
            @pl.when(a - d >= 0)
            def _():
                w_wait(kind, c - PAIR * d)

                @pl.when(has_right)
                def _():
                    w_copy(kind, a - d, 0).start()

                w_copy(kind, a - d, 2).start()

            @pl.when(a + d < line)
            def _():
                w_wait(kind, c + PAIR * d)

                @pl.when(has_left)
                def _():
                    w_copy(kind, a + d, 1).start()

                w_copy(kind, a + d, 2).start()

            return carry

        lax.fori_loop(1, line, body, 0)

    def pass_o():
        def body(d, carry):
            @pl.when(a - d >= 0)
            def _():
                o_line(a - d, 0).wait_recv()

                @pl.when(has_right)
                def _():
                    o_line(a - d, 0).start()

                o_route(a - d)

            @pl.when(a + d < line)
            def _():
                o_line(a + d, 1).wait_recv()

                @pl.when(has_left)
                def _():
                    o_line(a + d, 1).start()

                o_route(a + d)

            return carry

        lax.fori_loop(1, line, body, 0)

    def h_forward(i):
        for q in range(n_y):
            @pl.when(q != y)
            def _():
                slot = 2 * q + core
                h_copy(slot, i, hf_send.at[q, i], sib).wait_recv()
                h_copy(slot, i, hf_send.at[q, i], sib).start()

    def pair_wait(kind):
        def body(pa, carry):
            w_wait(kind, PAIR * pa + (1 - b))
            return carry

        lax.fori_loop(0, line, body, 0)

    own_sends(KINDS[0])
    for i in range(HIDDEN_CHUNKS):
        h_copy(t, i, hs_send.at[i], sib).start()
    own_sends(KINDS[1])
    pass_on(KINDS[0])
    own_sends(KINDS[2])
    pass_on(KINDS[1])
    h_forward(0)
    own_o()
    pass_on(KINDS[2])
    for i in range(1, HIDDEN_CHUNKS):
        h_forward(i)

    for i in range(HIDDEN_CHUNKS):
        h_copy(sib, i, hs_send.at[i], sib).wait_recv()
        for q in range(n_y):
            @pl.when(q != y)
            def _():
                h_copy(2 * q + 1 - core, i, hs_send.at[i], sib).wait_recv()

    def squares(p, sums):
        part = hbuf[p].astype(jnp.float32)
        return sums + jnp.sum(part * part, axis=1, keepdims=True)

    sums = lax.fori_loop(0, n_tp, squares, jnp.zeros((seg, 1), jnp.float32))
    scale[...] = jnp.broadcast_to(
        lax.rsqrt(sums / (own_d * n_tp) + 1e-06), scale.shape
    )

    def project(kinds):
        width = HD * len(kinds)

        def body(p, acc):
            w = [
                wbuf[k, pl.ds(PAIR * p, PAIR)].reshape(PAIR * depth, HD) for k in kinds
            ]
            w = w[0] if len(w) == 1 else jnp.concatenate(w, axis=1)
            return acc + jnp.dot(hbuf[p], w, preferred_element_type=jnp.float32)

        return lax.fori_loop(0, n_tp, body, jnp.zeros((seg, width), jnp.float32))

    pair_wait(1)
    pair_wait(2)
    proj = project((1, 2))
    kv[0] = (proj[:, :HD] * scale[...]).astype(jnp.bfloat16)
    kv[1] = (proj[:, HD:] * scale[...]).astype(jnp.bfloat16)

    def kv_copy(dest):
        return remote(kv, mem, kv_send, kv_recv, ctx=dest)

    @pl.when(c + 1 < n_ctx)
    def _():
        kv_copy(c + 1).start()

    pass_o()
    for p in range(n_tp):
        @pl.when(p != t)
        def _():
            part = wouse.at[b, pl.ds(p * HD, HD), :]
            remote(part, part, ot_send.at[0], ot_recv.at[p], tp=p).wait_recv()
            o_pair(p).start()

    pair_wait(0)
    qbuf[...] = (project((0,)) * scale[...] * (1.0 / math.sqrt(HD))).astype(jnp.bfloat16)

    @pl.when(c > 0)
    def _():
        kv_copy(c).wait_recv()

    q_rows = min(128, seg)
    mine = pl.ds(pl.multiple_of(t * HD, HD), HD)

    def attend(i, carry):
        rows = pl.ds(pl.multiple_of(i * q_rows, q_rows), q_rows)
        q = qbuf[rows, :]
        nt = (((1,), (1,)), ((), ()))
        s_mem = lax.dot_general(q, mem[0], nt, preferred_element_type=jnp.float32)
        s_own = lax.dot_general(q, kv[0], nt, preferred_element_type=jnp.float32)
        s_mem = jnp.where(c > 0, s_mem, -1e30)
        row = lax.broadcasted_iota(jnp.int32, s_own.shape, 0) + i * q_rows
        col = lax.broadcasted_iota(jnp.int32, s_own.shape, 1)
        s_own = jnp.where(col <= row, s_own, -1e30)
        top = jnp.maximum(
            jnp.max(s_mem, axis=1, keepdims=True), jnp.max(s_own, axis=1, keepdims=True)
        )
        e_mem = jnp.exp(s_mem - top)
        e_own = jnp.exp(s_own - top)
        total = jnp.sum(e_mem, axis=1, keepdims=True) + jnp.sum(e_own, axis=1, keepdims=True)
        mixed = jnp.dot(e_mem.astype(jnp.bfloat16), mem[1], preferred_element_type=jnp.float32)
        mixed += jnp.dot(e_own.astype(jnp.bfloat16), kv[1], preferred_element_type=jnp.float32)
        att[rows, mine] = (mixed / total).astype(jnp.bfloat16)
        return carry

    lax.fori_loop(0, seg // q_rows, attend, 0)

    def att_copy(head, dest):
        part = att.at[:, pl.ds(pl.multiple_of(head * HD, HD), HD)]
        return remote(part, part, a_send.at[dest], a_recv.at[head], tp=dest)

    for p in range(n_tp):
        @pl.when(p != t)
        def _():
            att_copy(t, p).start()

    for p in range(n_tp):
        @pl.when(p != t)
        def _():
            att_copy(p, p).wait_recv()
    for p in range(n_tp):
        part = wouse.at[1 - b, pl.ds(p * HD, HD), :]
        remote(part, part, ox_send.at[p], ox_recv.at[p], ctx=pair_c).wait_recv()

    wide = o_ref.shape[1]
    o_rows = min(128, seg)

    def final(i, carry):
        rows = pl.ds(pl.multiple_of(i * o_rows, o_rows), o_rows)
        for r in range(PAIR):
            cols = pl.ds(r * wide, wide)
            branch = jnp.dot(att[rows, :], wouse[r], preferred_element_type=jnp.float32)
            out_ref[rows, cols] = (hid_ref[rows, cols].astype(jnp.float32) + branch).astype(
                out_ref.dtype
            )
        return carry

    lax.fori_loop(0, seg // o_rows, final, 0)

    for i in range(HIDDEN_CHUNKS):
        h_copy(t, i, hs_send.at[i], sib).wait_send()
        for q in range(n_y):
            @pl.when(q != y)
            def _():
                h_copy(t, i, hy_send.at[q, i], 2 * q + core).wait_send()
                h_copy(2 * q + core, i, hf_send.at[q, i], sib).wait_send()

    def drain(pa, carry):
        right = has_right & (pa <= a)
        left = has_left & (pa >= a)
        for kind in KINDS:
            w_copy(kind, pa, 2).wait_send()

        @pl.when(right)
        def _():
            for kind in KINDS:
                w_copy(kind, pa, 0).wait_send()
            o_line(pa, 0).wait_send()

        @pl.when(left)
        def _():
            for kind in KINDS:
                w_copy(kind, pa, 1).wait_send()
            o_line(pa, 1).wait_send()

        @pl.when(pa != t)
        def _():
            o_tp(pa).wait_send()

        return carry

    lax.fori_loop(0, line, drain, 0)
    for p in range(n_tp):
        o_pair(p).wait_send()

        @pl.when(p != t)
        def _():
            att_copy(t, p).wait_send()

    @pl.when(c + 1 < n_ctx)
    def _():
        kv_copy(c + 1).wait_send()


def per_device(n_ctx, n_tp, hidden, norm_gain, w_qkv, w_out):
    seg, own_d = hidden.shape
    _, kinds, depth, head = w_qkv.shape
    wide = w_out.shape[2]
    line, n_y = n_ctx // PAIR, n_tp // 2
    bf16, f32 = jnp.bfloat16, jnp.float32
    dma = pltpu.SemaphoreType.DMA
    vmem = pl.BlockSpec(memory_space=pltpu.VMEM)
    flops = 2 * seg * own_d * n_tp * 3 * HD + 8 * seg * seg * HD + 2 * seg * HD * n_tp * own_d
    return pl.pallas_call(
        functools.partial(kernel, n_ctx, n_tp),
        out_shape=jax.ShapeDtypeStruct((seg, own_d), hidden.dtype),
        in_specs=[vmem] * 4,
        out_specs=vmem,
        scratch_shapes=[
            pltpu.VMEM((n_tp, seg, own_d), bf16),
            pltpu.VMEM((kinds, n_ctx, depth, head), bf16),
            pltpu.VMEM((line, head, wide), bf16),
            pltpu.VMEM((PAIR, n_tp * head, wide), bf16),
            pltpu.VMEM((2, seg, head), bf16),
            pltpu.VMEM((2, seg, head), bf16),
            pltpu.VMEM((seg, head), bf16),
            pltpu.VMEM((seg, n_tp * head), bf16),
            pltpu.VMEM((seg, head), f32),
            dma((kinds, n_ctx)),
            dma((kinds, line, 3)),
            dma((line,)),
            dma((line, 2)),
            dma((n_tp,)),
            dma((line,)),
            dma((n_tp,)),
            dma((n_tp,)),
            dma((n_tp, HIDDEN_CHUNKS)),
            dma((HIDDEN_CHUNKS,)),
            dma((n_y, HIDDEN_CHUNKS)),
            dma((n_y, HIDDEN_CHUNKS)),
            dma,
            dma,
            dma((n_tp,)),
            dma((n_tp,)),
        ],
        compiler_params=pltpu.CompilerParams(
            collective_id=0, has_side_effects=True, vmem_limit_bytes=48 * 1024 * 1024
        ),
        cost_estimate=pl.CostEstimate(
            flops=flops, bytes_accessed=4 * seg * own_d, transcendentals=2 * seg * seg
        ),
    )(hidden, norm_gain, w_qkv[0], w_out[0])


def solution(mesh):
    n_ctx, n_tp = mesh.shape["ctx"], mesh.shape["tp"]
    placed = (P("ctx", "tp"), P(None, "ctx"), P(None, None, "ctx", "tp"), P(None, "tp", "ctx"))
    return jax.shard_map(
        functools.partial(per_device, n_ctx, n_tp),
        mesh=mesh, in_specs=placed, out_specs=P("ctx", "tp"), check_vma=False,
    )
```

time: 209 us -> 65.2 us (0.31); the launches traced: 206 us -> 65 us
  waiting for transfers between devices: 153 us -> 0 us
  Pallas kernels: 0 us -> 60.2 us
  blocking collectives: 20.5 us -> 0 us
  between operations: 13.2 us -> 0.01 us
  matrix products: 11.7 us -> 0 us
  other arithmetic: 5.71 us -> 0 us
  local copies, waits for them, and re-layouts: 0.06 us -> 4.78 us
    all_gather x3 -> x0, waiting for transfers between devices: 96.1 us -> none  [the longest x1 57.9 us: project_rows(): piece_w = lax.all_gather(weights, 'ctx', axis=1, tiled=True)]
    pallas_call x0 -> x1, Pallas kernels: none -> 60.2 us  [per_device(): pl.pallas_call(functools.partial(kernel, n_ctx, n_tp), out_shape=jax.Shap...]
    reduce_scatter x1 -> x0, waiting for transfers between devices: 46 us -> none  [per_device(): lax.psum_scatter(partials.astype(jnp.bfloat16), 'tp', scatter_dimension=1...]
    all_gather x1 -> x0, blocking collectives: 20.5 us -> none  [project_rows(): piece_g = lax.all_gather(row_gain, 'ctx', axis=1, tiled=True)]
    dot_general x3 -> x0, matrix products: 11.7 us -> none  [the longest x1 5.54 us: project_rows(): jnp.einsum('rd,cdh->crh', inputs, piece_w, preferred_element_type=jnp.flo...]
    ppermute x1 -> x0, waiting for transfers between devices: 9.21 us -> none  [shifted(): return lax.ppermute(value, axis, pairs)]
    unnamed x2 -> x9, local copies, waits for them, and re-layouts: 0.01 us -> 4.78 us
    reduce_sum x1 -> x0, other arithmetic: 3.08 us -> none  [normalize(): jnp.mean(values * values, axis=-1, keepdims=True) + 1e-06]
  transfers between devices with their start and end apart: 5 -> 0, of which waited for: 5 -> 0; matrix products, arithmetic and copies ran while one was open for 5% -> 0% of each run, Pallas kernels for 0% -> 0%
where the time goes in v1:
time: 65.2 us; the launch traced here: 65 us
  Pallas kernels  60.2 us (92%)
  local copies, waits for them, and re-layouts  4.78 us (7%)
    pallas_call x1, Pallas kernels, per_device(): pl.pallas_call(functools.partial(kernel, n_ctx, n_tp), out_shape=jax.Shap...  60.2 us
    unnamed x9, local copies, waits for them, and re-layouts  4.78 us

profile of v1, /device:TPU:31, one launch (start us, length us, event | category | flops | bytes accessed | tf_op | source)
XLA Modules:
  0.0 65.0 jit_solution(13466744280262273921)
XLA Ops:
  0.0 0.0 copy-start.3
  0.0 0.7 %copy-done.3 = bf16[1,512]{1,0:T(2,128)(2,1)S(1)} copy-done((bf16[1,512]{1,0:T(2,128)(2,1)S(1)}, bf16[1,512]{1,0:T(2,128)(2,1)}, u32[]{:S(2)}) %copy-start.3) | copy-done | bytes 1048
  0.7 0.0 copy-start
  0.7 1.2 %copy-done = bf16[512,1024]{1,0:T(8,128)(2,1)S(1)} copy-done((bf16[512,1024]{1,0:T(8,128)(2,1)S(1)}, bf16[512,1024]{1,0:T(8,128)(2,1)}, u32[]{:S(2)}) %copy-start) | copy-done | bytes 1048600
  1.9 0.0 copy-start.1
  1.9 1.0 %copy-done.1 = bf16[1,3,512,128]{3,2,1,0:T(8,128)(2,1)S(1)} copy-done((bf16[1,3,512,128]{3,2,1,0:T(8,128)(2,1)S(1)}, bf16[1,3,512,128]{3,2,1,0:T(8,128)(2,1)}, u32[]{:S(2)}) %copy-start.1) | copy-done | bytes 393240
  2.9 0.0 copy-start.2
  2.9 0.9 %copy-done.2 = bf16[1,128,512]{2,1,0:T(8,128)(2,1)S(1)} copy-done((bf16[1,128,512]{2,1,0:T(8,128)(2,1)S(1)}, bf16[1,128,512]{2,1,0:T(8,128)(2,1)}, u32[]{:S(2)}) %copy-start.2) | copy-done | bytes 131096
  3.8 60.2 %shard_map.46 = bf16[512,1024]{1,0:T(8,128)(2,1)S(1)} custom-call(bf16[512,1024]{1,0:T(8,128)(2,1)S(1)} %copy-done, bf16[1,512]{1,0:T(2,128)(2,1)S(1)} %copy-done.3, bf16[3,512,128]{2,1,0:T(8,128)(2,1)S(1)} %bitcast.2, bf16[128,512]{1,0:T(8,128)(2,1)S(1)} %bitcast.3), custom_call_target="tpu_custom_call" | custom-call | flops 2415919104 | bytes 2097152 | tf_op jit(solution)/shard_map/pallas_call | solution.py:409
  64.0 1.0 %copy.6 = bf16[512,1024]{1,0:T(8,128)(2,1)} copy(bf16[512,1024]{1,0:T(8,128)(2,1)S(1)} %shard_map.46) | data formatting | bytes 2097152
Async XLA Ops:
  0.0 0.7 %copy-start.3 = (bf16[1,512]{1,0:T(2,128)(2,1)S(1)}, bf16[1,512]{1,0:T(2,128)(2,1)}, u32[]{:S(2)}) copy-start(bf16[1,512]{1,0:T(2,128)(2,1)} %gain_ref.1) | copy-start | bytes 3076
  0.7 1.2 %copy-start = (bf16[512,1024]{1,0:T(8,128)(2,1)S(1)}, bf16[512,1024]{1,0:T(8,128)(2,1)}, u32[]{:S(2)}) copy-start(bf16[512,1024]{1,0:T(8,128)(2,1)} %hid_ref.1) | copy-start | bytes 3145732
  1.9 1.0 %copy-start.1 = (bf16[1,3,512,128]{3,2,1,0:T(8,128)(2,1)S(1)}, bf16[1,3,512,128]{3,2,1,0:T(8,128)(2,1)}, u32[]{:S(2)}) copy-start(bf16[1,3,512,128]{3,2,1,0:T(8,128)(2,1)} %param.6) | copy-start | bytes 1179652
  2.9 0.9 %copy-start.2 = (bf16[1,128,512]{2,1,0:T(8,128)(2,1)S(1)}, bf16[1,128,512]{2,1,0:T(8,128)(2,1)}, u32[]{:S(2)}) copy-start(bf16[1,128,512]{2,1,0:T(8,128)(2,1)} %param.7) | copy-start | bytes 393220

commit v2 on v1

--- a/solution.py
+++ b/solution.py
@@ -11,15 +11,16 @@
 HD = 128
 PAIR = 2
 HIDDEN_CHUNKS = 2
+ATT_CHUNKS = 2
 KINDS = (1, 2, 0)
 
 
 def kernel(
     n_ctx, n_tp,
     hid_ref, gain_ref, w_ref, o_ref, out_ref,
-    hbuf, wbuf, obuf, wouse, kv, mem, qbuf, att, scale,
+    wstage, gstage, ostage, hbuf, wbuf, obuf, wouse, kv, mem, qbuf, att, scale,
     w_recv, w_send, ol_recv, ol_send, ot_recv, ot_send, ox_recv, ox_send,
-    h_recv, hs_send, hy_send, hf_send, kv_recv, kv_send, a_recv, a_send,
+    h_recv, hs_send, hy_send, hf_send, kv_recv, kv_send, a_recv, a_send, in_sem, out_sem,
 ):
     line = n_ctx // PAIR
     n_y = n_tp // 2
@@ -30,7 +31,7 @@
     y = lax.div(t, 2)
     core = lax.rem(t, 2)
     seg, own_d = hid_ref.shape
-    depth = w_ref.shape[1]
+    depth = w_ref.shape[2]
     rows_c = seg // HIDDEN_CHUNKS
     pair_c = PAIR * a + (1 - b)
     sib = 2 * y + (1 - core)
@@ -48,6 +49,15 @@
             device_id=where, device_id_type=pl.DeviceIdType.MESH,
         )
 
+    loads = [
+        pltpu.make_async_copy(gain_ref, gstage, in_sem.at[0]),
+        pltpu.make_async_copy(w_ref.at[0], wstage, in_sem.at[1]),
+        pltpu.make_async_copy(hid_ref, hbuf.at[t], in_sem.at[2]),
+        pltpu.make_async_copy(o_ref.at[0], obuf.at[a], in_sem.at[3]),
+    ]
+    for load in loads:
+        load.start()
+
     barrier = pltpu.get_barrier_semaphore()
 
     def greet(**where):
@@ -75,11 +85,13 @@
     def _():
         greet(ctx=c - 1)
 
-    gain = jnp.transpose(jnp.broadcast_to(gain_ref[...].astype(jnp.float32), (HD, depth)))
+    loads[0].wait()
+    loads[1].wait()
+    gain = jnp.transpose(jnp.broadcast_to(gstage[...].astype(jnp.float32), (HD, depth)))
     for kind in KINDS:
-        wbuf[kind, c] = (w_ref[kind].astype(jnp.float32) * gain).astype(jnp.bfloat16)
-    obuf[a] = o_ref[...]
-    hbuf[t] = hid_ref[...]
+        wbuf[kind, c] = (wstage[kind].astype(jnp.float32) * gain).astype(jnp.bfloat16)
+    loads[2].wait()
+    loads[3].wait()
 
     @pl.when(c == 0)
     def _():
@@ -103,11 +115,10 @@
             def _():
                 h_copy(t, i, hy_send.at[q, i], 2 * q + core).start()
 
-    def w_copy(kind, pa, way):
-        pc = PAIR * pa + b
+    def w_copy(kind, pc, way):
         slot = wbuf.at[kind, pc]
         dest = (c + PAIR, c - PAIR, pair_c)[way]
-        return remote(slot, slot, w_send.at[kind, pa, way], w_recv.at[kind, pc], ctx=dest)
+        return remote(slot, slot, w_send.at[kind, pc, way], w_recv.at[kind, pc], ctx=dest)
 
     def o_line(pa, way):
         slot = obuf.at[pa]
@@ -122,16 +133,14 @@
         part = wouse.at[b, pl.ds(pl.multiple_of(head * HD, HD), HD), :]
         return remote(part, part, ox_send.at[head], ox_recv.at[head], ctx=pair_c)
 
-    def own_sends(kind):
+    def line_sends(kind, pc):
         @pl.when(has_right)
         def _():
-            w_copy(kind, a, 0).start()
+            w_copy(kind, pc, 0).start()
 
         @pl.when(has_left)
         def _():
-            w_copy(kind, a, 1).start()
-
-        w_copy(kind, a, 2).start()
+            w_copy(kind, pc, 1).start()
 
     def own_o():
         @pl.when(has_right)
@@ -155,36 +164,57 @@
             o_tp(pa).start()
 
     def w_wait(kind, pc):
-        slot = wbuf.at[kind, pc]
-        remote(slot, slot, w_send.at[kind, 0, 0], w_recv.at[kind, pc], ctx=pair_c).wait_recv()
-
-    def pass_on(kind):
+        w_copy(kind, pc, 2).wait_recv()
+
+    def pass_on(kind, first, last):
+        both = kind == KINDS[-1]
+        parities = (b, 1 - b) if both else (b,)
+
         def body(d, carry):
-            @pl.when(a - d >= 0)
-            def _():
-                w_wait(kind, c - PAIR * d)
-
-                @pl.when(has_right)
+            for parity in parities:
+                @pl.when(a - d >= 0)
                 def _():
-                    w_copy(kind, a - d, 0).start()
-
-                w_copy(kind, a - d, 2).start()
-
-            @pl.when(a + d < line)
-            def _():
-                w_wait(kind, c + PAIR * d)
-
-                @pl.when(has_left)
+                    pc = PAIR * (a - d) + parity
+                    w_wait(kind, pc)
+
+                    @pl.when(has_right)
+                    def _():
+                        w_copy(kind, pc, 0).start()
+
+                    if not both:
+                        w_copy(kind, pc, 2).start()
+
+                @pl.when(a + d < line)
                 def _():
-                    w_copy(kind, a + d, 1).start()
-
-                w_copy(kind, a + d, 2).start()
+                    pc = PAIR * (a + d) + parity
+                    w_wait(kind, pc)
+
+                    @pl.when(has_left)
+                    def _():
+                        w_copy(kind, pc, 1).start()
+
+                    if not both:
+                        w_copy(kind, pc, 2).start()
 
             return carry
 
-        lax.fori_loop(1, line, body, 0)
-
-    def pass_o():
+        lax.fori_loop(first, last, body, 0)
+
+    def o_forward(d):
+        @pl.when((a - t == d) | (t - a == d))
+        def _():
+            def one(p, carry):
+                @pl.when(p != t)
+                def _():
+                    part = wouse.at[b, pl.ds(pl.multiple_of(p * HD, HD), HD), :]
+                    remote(part, part, ot_send.at[0], ot_recv.at[p], tp=p).wait_recv()
+                    o_pair(p).start()
+
+                return carry
+
+            lax.fori_loop(0, n_tp, one, 0)
+
+    def pass_o(first, last):
         def body(d, carry):
             @pl.when(a - d >= 0)
             def _():
@@ -206,9 +236,10 @@
 
                 o_route(a + d)
 
+            o_forward(d - 1)
             return carry
 
-        lax.fori_loop(1, line, body, 0)
+        lax.fori_loop(first, last, body, 0)
 
     def h_forward(i):
         for q in range(n_y):
@@ -225,16 +256,22 @@
 
         lax.fori_loop(0, line, body, 0)
 
-    own_sends(KINDS[0])
+    kind_k, kind_v, kind_q = KINDS
+    line_sends(kind_k, c)
+    w_copy(kind_k, c, 2).start()
+    w_copy(kind_q, c, 2).start()
     for i in range(HIDDEN_CHUNKS):
         h_copy(t, i, hs_send.at[i], sib).start()
-    own_sends(KINDS[1])
-    pass_on(KINDS[0])
-    own_sends(KINDS[2])
-    pass_on(KINDS[1])
+    line_sends(kind_v, c)
+    w_copy(kind_v, c, 2).start()
+    pass_on(kind_k, 1, line)
+    line_sends(kind_q, c)
+    w_wait(kind_q, pair_c)
+    line_sends(kind_q, pair_c)
+    pass_on(kind_v, 1, line)
     h_forward(0)
     own_o()
-    pass_on(KINDS[2])
+    pass_on(kind_q, 1, line - 1)
     for i in range(1, HIDDEN_CHUNKS):
         h_forward(i)
 
@@ -279,15 +316,8 @@
     def _():
         kv_copy(c + 1).start()
 
-    pass_o()
-    for p in range(n_tp):
-        @pl.when(p != t)
-        def _():
-            part = wouse.at[b, pl.ds(p * HD, HD), :]
-            remote(part, part, ot_send.at[0], ot_recv.at[p], tp=p).wait_recv()
-            o_pair(p).start()
-
-    pair_wait(0)
+    pass_on(kind_q, line - 1, line)
+    pass_o(1, 2)
     qbuf[...] = (project((0,)) * scale[...] * (1.0 / math.sqrt(HD))).astype(jnp.bfloat16)
 
     @pl.when(c > 0)
@@ -318,26 +348,34 @@
         att[rows, mine] = (mixed / total).astype(jnp.bfloat16)
         return carry
 
-    lax.fori_loop(0, seg // q_rows, attend, 0)
-
-    def att_copy(head, dest):
-        part = att.at[:, pl.ds(pl.multiple_of(head * HD, HD), HD)]
-        return remote(part, part, a_send.at[dest], a_recv.at[head], tp=dest)
-
-    for p in range(n_tp):
-        @pl.when(p != t)
-        def _():
-            att_copy(t, p).start()
-
-    for p in range(n_tp):
-        @pl.when(p != t)
-        def _():
-            att_copy(p, p).wait_recv()
+    a_rows = seg // ATT_CHUNKS
+
+    def att_copy(head, dest, i):
+        part = att.at[pl.ds(i * a_rows, a_rows), pl.ds(pl.multiple_of(head * HD, HD), HD)]
+        return remote(part, part, a_send.at[dest, i], a_recv.at[head, i], tp=dest)
+
+    for i in range(ATT_CHUNKS):
+        blocks = a_rows // q_rows
+        lax.fori_loop(i * blocks, (i + 1) * blocks, attend, 0)
+        for p in range(n_tp):
+            @pl.when(p != t)
+            def _():
+                att_copy(t, p, i).start()
+
+        steps = line - 2
+        pass_o(2 + steps * i // ATT_CHUNKS, 2 + steps * (i + 1) // ATT_CHUNKS)
+
+    o_forward(line - 1)
+    for i in range(ATT_CHUNKS):
+        for p in range(n_tp):
+            @pl.when(p != t)
+            def _():
+                att_copy(p, p, i).wait_recv()
     for p in range(n_tp):
         part = wouse.at[1 - b, pl.ds(p * HD, HD), :]
         remote(part, part, ox_send.at[p], ox_recv.at[p], ctx=pair_c).wait_recv()
 
-    wide = o_ref.shape[1]
+    wide = o_ref.shape[2]
     o_rows = min(128, seg)
 
     def final(i, carry):
@@ -345,9 +383,10 @@
         for r in range(PAIR):
             cols = pl.ds(r * wide, wide)
             branch = jnp.dot(att[rows, :], wouse[r], preferred_element_type=jnp.float32)
-            out_ref[rows, cols] = (hid_ref[rows, cols].astype(jnp.float32) + branch).astype(
+            ostage[rows, cols] = (hbuf[t, rows, cols].astype(jnp.float32) + branch).astype(
                 out_ref.dtype
             )
+        pltpu.make_async_copy(ostage.at[rows, :], out_ref.at[rows, :], out_sem.at[i]).start()
         return carry
 
     lax.fori_loop(0, seg // o_rows, final, 0)
@@ -360,41 +399,60 @@
                 h_copy(t, i, hy_send.at[q, i], 2 * q + core).wait_send()
                 h_copy(2 * q + core, i, hf_send.at[q, i], sib).wait_send()
 
-    def drain(pa, carry):
+    def drain(pc, carry):
+        pa, parity = lax.div(pc, PAIR), lax.rem(pc, PAIR)
         right = has_right & (pa <= a)
         left = has_left & (pa >= a)
-        for kind in KINDS:
-            w_copy(kind, pa, 2).wait_send()
+        same = parity == b
 
         @pl.when(right)
         def _():
-            for kind in KINDS:
-                w_copy(kind, pa, 0).wait_send()
-            o_line(pa, 0).wait_send()
+            w_copy(kind_q, pc, 0).wait_send()
 
         @pl.when(left)
         def _():
-            for kind in KINDS:
-                w_copy(kind, pa, 1).wait_send()
-            o_line(pa, 1).wait_send()
-
-        @pl.when(pa != t)
-        def _():
-            o_tp(pa).wait_send()
+            w_copy(kind_q, pc, 1).wait_send()
+
+        @pl.when(same)
+        def _():
+            w_copy(kind_k, pc, 2).wait_send()
+            w_copy(kind_v, pc, 2).wait_send()
+
+            @pl.when(right)
+            def _():
+                w_copy(kind_k, pc, 0).wait_send()
+                w_copy(kind_v, pc, 0).wait_send()
+                o_line(pa, 0).wait_send()
+
+            @pl.when(left)
+            def _():
+                w_copy(kind_k, pc, 1).wait_send()
+                w_copy(kind_v, pc, 1).wait_send()
+                o_line(pa, 1).wait_send()
+
+            @pl.when(pa != t)
+            def _():
+                o_tp(pa).wait_send()
 
         return carry
 
-    lax.fori_loop(0, line, drain, 0)
+    lax.fori_loop(0, n_ctx, drain, 0)
+    w_copy(kind_q, c, 2).wait_send()
     for p in range(n_tp):
         o_pair(p).wait_send()
 
         @pl.when(p != t)
         def _():
-            att_copy(t, p).wait_send()
+            for i in range(ATT_CHUNKS):
+                att_copy(t, p, i).wait_send()
 
     @pl.when(c + 1 < n_ctx)
     def _():
         kv_copy(c + 1).wait_send()
+
+    for i in range(seg // o_rows):
+        rows = pl.ds(i * o_rows, o_rows)
+        pltpu.make_async_copy(ostage.at[rows, :], out_ref.at[rows, :], out_sem.at[i]).wait()
 
 
 def per_device(n_ctx, n_tp, hidden, norm_gain, w_qkv, w_out):
@@ -404,14 +462,17 @@
     line, n_y = n_ctx // PAIR, n_tp // 2
     bf16, f32 = jnp.bfloat16, jnp.float32
     dma = pltpu.SemaphoreType.DMA
-    vmem = pl.BlockSpec(memory_space=pltpu.VMEM)
+    hbm = pl.BlockSpec(memory_space=pl.ANY)
     flops = 2 * seg * own_d * n_tp * 3 * HD + 8 * seg * seg * HD + 2 * seg * HD * n_tp * own_d
     return pl.pallas_call(
         functools.partial(kernel, n_ctx, n_tp),
         out_shape=jax.ShapeDtypeStruct((seg, own_d), hidden.dtype),
-        in_specs=[vmem] * 4,
-        out_specs=vmem,
+        in_specs=[hbm] * 4,
+        out_specs=hbm,
         scratch_shapes=[
+            pltpu.VMEM((kinds, depth, head), bf16),
+            pltpu.VMEM(norm_gain.shape, bf16),
+            pltpu.VMEM((seg, own_d), bf16),
             pltpu.VMEM((n_tp, seg, own_d), bf16),
             pltpu.VMEM((kinds, n_ctx, depth, head), bf16),
             pltpu.VMEM((line, head, wide), bf16),
@@ -422,7 +483,7 @@
             pltpu.VMEM((seg, n_tp * head), bf16),
             pltpu.VMEM((seg, head), f32),
             dma((kinds, n_ctx)),
-            dma((kinds, line, 3)),
+            dma((kinds, n_ctx, 3)),
             dma((line,)),
             dma((line, 2)),
             dma((n_tp,)),
@@ -435,16 +496,18 @@
             dma((n_y, HIDDEN_CHUNKS)),
             dma,
             dma,
-            dma((n_tp,)),
-            dma((n_tp,)),
+            dma((n_tp, ATT_CHUNKS)),
+            dma((n_tp, ATT_CHUNKS)),
+            dma((4,)),
+            dma((seg // min(128, seg),)),
         ],
         compiler_params=pltpu.CompilerParams(
-            collective_id=0, has_side_effects=True, vmem_limit_bytes=48 * 1024 * 1024
+            collective_id=0, has_side_effects=True, vmem_limit_bytes=56 * 1024 * 1024
         ),
         cost_estimate=pl.CostEstimate(
             flops=flops, bytes_accessed=4 * seg * own_d, transcendentals=2 * seg * seg
         ),
-    )(hidden, norm_gain, w_qkv[0], w_out[0])
+    )(hidden, norm_gain, w_qkv, w_out)
 
 
 def solution(mesh):

time: 65.2 us -> 74.5 us (1.14)
  the two profiles are of different devices: /device:TPU:31 before, /device:TPU:5 now
where the time goes in v2:
time: 74.5 us; the launch traced here: 74.3 us
  Pallas kernels  72 us (97%)
  local copies, waits for them, and re-layouts  2.26 us (3%)
    pallas_call x1, Pallas kernels, per_device(): pl.pallas_call(functools.partial(kernel, n_ctx, n_tp), out_shape=jax.Shap...  72 us
    unnamed x1, local copies, waits for them, and re-layouts  2.26 us

profile of v2, /device:TPU:5, one launch (start us, length us, event | category | flops | bytes accessed | tf_op | source)
XLA Modules:
  0.0 74.3 jit_solution(13138997565323701948)
XLA Ops:
  0.0 72.0 %shard_map.46 = bf16[512,1024]{1,0:T(8,128)(2,1)} custom-call(bf16[512,1024]{1,0:T(8,128)(2,1)} %hid_ref.1, bf16[1,512]{1,0:T(2,128)(2,1)} %gain_ref.1, bf16[1,3,512,128]{3,2,1,0:T(8,128)(2,1)} %w_ref.1, bf16[1,128,512]{2,1,0:T(8,128)(2,1)} %o_ref.1), custom_call_target="tpu_custom_call" | custom-call | flops 2415919104 | bytes 2097152 | tf_op jit(solution)/shard_map/pallas_call | solution.py:467
  72.1 2.3 %copy.6 = bf16[512,1024]{1,0:T(8,128)(2,1)} copy(bf16[512,1024]{1,0:T(8,128)(2,1)} %shard_map.46) | data formatting | bytes 2097152

commit v3 on v2

--- a/solution.py
+++ b/solution.py
@@ -236,7 +236,10 @@
 
                 o_route(a + d)
 
-            o_forward(d - 1)
+            @pl.when(d > 1)
+            def _():
+                o_forward(d - 1)
+
             return carry
 
         lax.fori_loop(first, last, body, 0)
@@ -259,20 +262,20 @@
     kind_k, kind_v, kind_q = KINDS
     line_sends(kind_k, c)
     w_copy(kind_k, c, 2).start()
-    w_copy(kind_q, c, 2).start()
     for i in range(HIDDEN_CHUNKS):
         h_copy(t, i, hs_send.at[i], sib).start()
     line_sends(kind_v, c)
     w_copy(kind_v, c, 2).start()
     pass_on(kind_k, 1, line)
+    w_copy(kind_q, c, 2).start()
     line_sends(kind_q, c)
+    pass_on(kind_v, 1, line)
     w_wait(kind_q, pair_c)
     line_sends(kind_q, pair_c)
-    pass_on(kind_v, 1, line)
-    h_forward(0)
     own_o()
-    pass_on(kind_q, 1, line - 1)
-    for i in range(1, HIDDEN_CHUNKS):
+    pass_on(kind_q, 1, 2)
+    o_forward(0)
+    for i in range(HIDDEN_CHUNKS):
         h_forward(i)
 
     for i in range(HIDDEN_CHUNKS):
@@ -303,6 +306,7 @@
 
         return lax.fori_loop(0, n_tp, body, jnp.zeros((seg, width), jnp.float32))
 
+    pass_on(kind_q, 2, line - 1)
     pair_wait(1)
     pair_wait(2)
     proj = project((1, 2))
@@ -319,6 +323,7 @@
     pass_on(kind_q, line - 1, line)
     pass_o(1, 2)
     qbuf[...] = (project((0,)) * scale[...] * (1.0 / math.sqrt(HD))).astype(jnp.bfloat16)
+    pass_o(2, line - 1)
 
     @pl.when(c > 0)
     def _():
@@ -362,9 +367,7 @@
             def _():
                 att_copy(t, p, i).start()
 
-        steps = line - 2
-        pass_o(2 + steps * i // ATT_CHUNKS, 2 + steps * (i + 1) // ATT_CHUNKS)
-
+    pass_o(line - 1, line)
     o_forward(line - 1)
     for i in range(ATT_CHUNKS):
         for p in range(n_tp):

time: 74.5 us -> 73.5 us (0.987)
  the two profiles are of different devices: /device:TPU:5 before, /device:TPU:24 now
where the time goes in v3:
time: 73.5 us; the launch traced here: 73.3 us
  Pallas kernels  71.1 us (97%)
  local copies, waits for them, and re-layouts  2.26 us (3%)
    pallas_call x1, Pallas kernels, per_device(): pl.pallas_call(functools.partial(kernel, n_ctx, n_tp), out_shape=jax.Shap...  71.1 us
    unnamed x1, local copies, waits for them, and re-layouts  2.26 us

profile of v3, /device:TPU:24, one launch (start us, length us, event | category | flops | bytes accessed | tf_op | source)
XLA Modules:
  0.0 73.3 jit_solution(7722114380125046090)
XLA Ops:
  0.0 71.1 %shard_map.46 = bf16[512,1024]{1,0:T(8,128)(2,1)} custom-call(bf16[512,1024]{1,0:T(8,128)(2,1)} %hid_ref.1, bf16[1,512]{1,0:T(2,128)(2,1)} %gain_ref.1, bf16[1,3,512,128]{3,2,1,0:T(8,128)(2,1)} %w_ref.1, bf16[1,128,512]{2,1,0:T(8,128)(2,1)} %o_ref.1), custom_call_target="tpu_custom_call" | custom-call | flops 2415919104 | bytes 2097152 | tf_op jit(solution)/shard_map/pallas_call | solution.py:470
  71.1 2.3 %copy.6 = bf16[512,1024]{1,0:T(8,128)(2,1)} copy(bf16[512,1024]{1,0:T(8,128)(2,1)} %shard_map.46) | data formatting | bytes 2097152

commit v4 on v3

--- a/solution.py
+++ b/solution.py
@@ -18,7 +18,7 @@
 def kernel(
     n_ctx, n_tp,
     hid_ref, gain_ref, w_ref, o_ref, out_ref,
-    wstage, gstage, ostage, hbuf, wbuf, obuf, wouse, kv, mem, qbuf, att, scale,
+    wstage, gstage, ostage, hbuf, wbuf, obuf, wouse, kv, mem, qbuf, att, scale, qacc,
     w_recv, w_send, ol_recv, ol_send, ot_recv, ot_send, ox_recv, ox_send,
     h_recv, hs_send, hy_send, hf_send, kv_recv, kv_send, a_recv, a_send, in_sem, out_sem,
 ):
@@ -200,19 +200,17 @@
 
         lax.fori_loop(first, last, body, 0)
 
-    def o_forward(d):
-        @pl.when((a - t == d) | (t - a == d))
-        def _():
-            def one(p, carry):
-                @pl.when(p != t)
-                def _():
-                    part = wouse.at[b, pl.ds(pl.multiple_of(p * HD, HD), HD), :]
-                    remote(part, part, ot_send.at[0], ot_recv.at[p], tp=p).wait_recv()
-                    o_pair(p).start()
-
-                return carry
-
-            lax.fori_loop(0, n_tp, one, 0)
+    def o_forward():
+        def one(p, carry):
+            @pl.when(p != t)
+            def _():
+                part = wouse.at[b, pl.ds(pl.multiple_of(p * HD, HD), HD), :]
+                remote(part, part, ot_send.at[0], ot_recv.at[p], tp=p).wait_recv()
+                o_pair(p).start()
+
+            return carry
+
+        lax.fori_loop(0, n_tp, one, 0)
 
     def pass_o(first, last):
         def body(d, carry):
@@ -235,10 +233,6 @@
                     o_line(a + d, 1).start()
 
                 o_route(a + d)
-
-            @pl.when(d > 1)
-            def _():
-                o_forward(d - 1)
 
             return carry
 
@@ -260,6 +254,7 @@
         lax.fori_loop(0, line, body, 0)
 
     kind_k, kind_v, kind_q = KINDS
+    w_copy(kind_q, c, 2).start()
     line_sends(kind_k, c)
     w_copy(kind_k, c, 2).start()
     for i in range(HIDDEN_CHUNKS):
@@ -267,14 +262,13 @@
     line_sends(kind_v, c)
     w_copy(kind_v, c, 2).start()
     pass_on(kind_k, 1, line)
-    w_copy(kind_q, c, 2).start()
+    own_o()
+    pass_on(kind_v, 1, line)
     line_sends(kind_q, c)
-    pass_on(kind_v, 1, line)
     w_wait(kind_q, pair_c)
     line_sends(kind_q, pair_c)
-    own_o()
+    pass_o(1, line)
     pass_on(kind_q, 1, 2)
-    o_forward(0)
     for i in range(HIDDEN_CHUNKS):
         h_forward(i)
 
@@ -306,7 +300,6 @@
 
         return lax.fori_loop(0, n_tp, body, jnp.zeros((seg, width), jnp.float32))
 
-    pass_on(kind_q, 2, line - 1)
     pair_wait(1)
     pair_wait(2)
     proj = project((1, 2))
@@ -320,10 +313,29 @@
     def _():
         kv_copy(c + 1).start()
 
+    pass_on(kind_q, 2, line - 1)
+    o_forward()
+
+    def q_block(p):
+        w = wbuf[kind_q, pl.ds(PAIR * p, PAIR)].reshape(PAIR * depth, HD)
+        qacc[...] += jnp.dot(hbuf[p], w, preferred_element_type=jnp.float32)
+
+    def q_blocks(d, carry):
+        @pl.when(a - d >= 0)
+        def _():
+            q_block(a - d)
+
+        @pl.when((a + d < line) & (d > 0))
+        def _():
+            q_block(a + d)
+
+        return carry
+
+    qacc[...] = jnp.zeros_like(qacc)
+    lax.fori_loop(0, line - 1, q_blocks, 0)
     pass_on(kind_q, line - 1, line)
-    pass_o(1, 2)
-    qbuf[...] = (project((0,)) * scale[...] * (1.0 / math.sqrt(HD))).astype(jnp.bfloat16)
-    pass_o(2, line - 1)
+    q_blocks(line - 1, 0)
+    qbuf[...] = (qacc[...] * scale[...] * (1.0 / math.sqrt(HD))).astype(jnp.bfloat16)
 
     @pl.when(c > 0)
     def _():
@@ -367,13 +379,6 @@
             def _():
                 att_copy(t, p, i).start()
 
-    pass_o(line - 1, line)
-    o_forward(line - 1)
-    for i in range(ATT_CHUNKS):
-        for p in range(n_tp):
-            @pl.when(p != t)
-            def _():
-                att_copy(p, p, i).wait_recv()
     for p in range(n_tp):
         part = wouse.at[1 - b, pl.ds(p * HD, HD), :]
         remote(part, part, ox_send.at[p], ox_recv.at[p], ctx=pair_c).wait_recv()
@@ -392,7 +397,13 @@
         pltpu.make_async_copy(ostage.at[rows, :], out_ref.at[rows, :], out_sem.at[i]).start()
         return carry
 
-    lax.fori_loop(0, seg // o_rows, final, 0)
+    for i in range(ATT_CHUNKS):
+        for p in range(n_tp):
+            @pl.when(p != t)
+            def _():
+                att_copy(p, p, i).wait_recv()
+        blocks = a_rows // o_rows
+        lax.fori_loop(i * blocks, (i + 1) * blocks, final, 0)
 
     for i in range(HIDDEN_CHUNKS):
         h_copy(t, i, hs_send.at[i], sib).wait_send()
@@ -485,6 +496,7 @@
             pltpu.VMEM((seg, head), bf16),
             pltpu.VMEM((seg, n_tp * head), bf16),
             pltpu.VMEM((seg, head), f32),
+            pltpu.VMEM((seg, head), f32),
             dma((kinds, n_ctx)),
             dma((kinds, n_ctx, 3)),
             dma((line,)),

time: 73.5 us -> 64.3 us (0.87)
  the two profiles are of different devices: /device:TPU:24 before, /device:TPU:31 now
where the time goes in v4:
time: 64.3 us; the launch traced here: 64.2 us
  Pallas kernels  61.9 us (96%)
  local copies, waits for them, and re-layouts  2.26 us (4%)
    pallas_call x1, Pallas kernels, per_device(): pl.pallas_call(functools.partial(kernel, n_ctx, n_tp), out_shape=jax.Shap...  61.9 us
    unnamed x1, local copies, waits for them, and re-layouts  2.26 us

profile of v4, /device:TPU:31, one launch (start us, length us, event | category | flops | bytes accessed | tf_op | source)
XLA Modules:
  0.0 64.2 jit_solution(12341710270942829823)
XLA Ops:
  0.0 61.9 %shard_map.46 = bf16[512,1024]{1,0:T(8,128)(2,1)} custom-call(bf16[512,1024]{1,0:T(8,128)(2,1)} %hid_ref.1, bf16[1,512]{1,0:T(2,128)(2,1)} %gain_ref.1, bf16[1,3,512,128]{3,2,1,0:T(8,128)(2,1)} %w_ref.1, bf16[1,128,512]{2,1,0:T(8,128)(2,1)} %o_ref.1), custom_call_target="tpu_custom_call" | custom-call | flops 2415919104 | bytes 2097152 | tf_op jit(solution)/shard_map/pallas_call | solution.py:481
  61.9 2.3 %copy.6 = bf16[512,1024]{1,0:T(8,128)(2,1)} copy(bf16[512,1024]{1,0:T(8,128)(2,1)} %shard_map.46) | data formatting | bytes 2097152
